TPU v7x, 256 devices: a whole 4x4x8 slice. The times are simulated.
256 devices in a mesh: dp: 32 (over z, x_lo, core), fsdp: 8 (over x_hi, y).
Axes of the slice: x: 4 (x_hi: 2, x_lo: 2; x = x_hi * 2 + x_lo), y: 4, z: 8, core: 2. Of those that a mesh axis runs over, the one named last changes fastest.
Arguments:
- grads: bfloat16 [32, 2, 8192, 1024], P('dp', None, 'fsdp'), may hold values from -1.1953125 to 1.1953125
- raw_proj: float32 [2, 1024, 512], P(None, 'fsdp'), may hold values from -6 to 6
- bucket_owner: int32 [2, 512], P(None, 'fsdp'), may hold values from 0 to 31, as said below
- first_moment: float32 [2, 8, 128, 16, 512], P(None, 'fsdp', 'dp'), may hold values from -0.6 to 0.6
- second_moment: float32 [2, 8, 128, 16, 512], P(None, 'fsdp', 'dp'), may hold values from 0.01 to 0.05
Outputs:
- weight_delta: bfloat16 [2, 8192, 1024], P(None, 'fsdp')
- first_out: float32 [2, 8, 128, 16, 512], P(None, 'fsdp', 'dp')
- second_out: float32 [2, 8, 128, 16, 512], P(None, 'fsdp', 'dp')
Inputs may be any that keep to these rules, and one draw needn't show every extreme that they name: `bucket_owner`: within each matrix and each block of 64 buckets of one fsdp index, no owner holds more than 4 buckets, and one owner holds exactly 4.
All inputs are finite; a program needn't handle non-finite values.
Results may differ from a plain program's by a relative error of at most 0.0062.
Values may be sent and summed in bfloat16 or wider, within the bound.
A program may use at most 64 MiB of HBM per device.

v0:
```python
import jax
import jax.numpy as jnp
from jax import lax
from jax.sharding import PartitionSpec as P


def rows_at(table, index):
    return jax.vmap(lambda part_table, part_index: jnp.take(part_table, part_index, axis=0))(
        table, index
    )


def adam_update(first, second, grad_rows):
    new_first = 0.9 * first + 0.1 * grad_rows
    new_second = 0.999 * second + 0.001 * grad_rows * grad_rows
    scaled = (
        6.0 * (new_first / (1.0 - 0.9**10)) / (jnp.sqrt(new_second / (1.0 - 0.999**10)) + 1e-08)
    )
    return (new_first, new_second, scaled.astype(jnp.bfloat16))


def shards(grads, raw_proj, bucket_owner, first_moment, second_moment):
    matrices = grads.shape[1]
    local_rows = grads.shape[2]
    features = grads.shape[3]
    rank_width = raw_proj.shape[2]
    buckets = bucket_owner.shape[1]
    capacity = first_moment.shape[2]
    bucket_rows = local_rows // buckets
    replicas = lax.axis_size("dp")
    slot_total = replicas * capacity
    gram_part = jnp.einsum("mkr,mks->mrs", raw_proj, raw_proj, precision=lax.Precision.HIGHEST)
    gram = lax.psum(gram_part, "fsdp")
    factor = jnp.linalg.cholesky(gram)
    basis_part = lax.linalg.triangular_solve(
        factor, raw_proj, left_side=False, lower=True, transpose_a=True
    )
    basis = lax.all_gather(basis_part.astype(jnp.bfloat16), "fsdp", axis=1, tiled=True)
    projected = jnp.einsum("mdk,mkr->mdr", grads[0], basis, preferred_element_type=jnp.float32)
    blocks = projected.reshape(matrices, buckets, bucket_rows, rank_width)
    same = bucket_owner[:, :, None] == bucket_owner[:, None, :]
    earlier = jnp.arange(buckets)[None, :] < jnp.arange(buckets)[:, None]
    ranks = jnp.sum(jnp.logical_and(same, earlier).astype(jnp.int32), axis=-1)
    slots = bucket_owner * capacity + ranks
    slot_ids = jnp.arange(slot_total, dtype=jnp.int32)
    matches = slots[:, None, :] == slot_ids[None, :, None]
    occupied = jnp.any(matches, axis=2)
    bucket_of = jnp.sum(
        matches.astype(jnp.int32) * jnp.arange(buckets, dtype=jnp.int32)[None, None, :], axis=2
    )
    start = lax.axis_index("dp") * capacity
    occupied_mine = lax.dynamic_slice_in_dim(occupied, start, capacity, 1)
    totals = lax.psum(blocks, "dp")
    bucket_mine = lax.dynamic_slice_in_dim(bucket_of, start, capacity, 1)
    grad_rows = rows_at(totals, bucket_mine)
    first = first_moment[:, 0]
    second = second_moment[:, 0]
    new_first, new_second, update = adam_update(first, second, grad_rows)
    keep_mask = occupied_mine[:, :, None, None]
    first_out = jnp.where(keep_mask, new_first, first)[:, None]
    second_out = jnp.where(keep_mask, new_second, second)[:, None]
    owner_rows = jnp.einsum(
        "mcbr,mkr->mcbk", update, basis, preferred_element_type=jnp.float32
    ).astype(jnp.bfloat16)
    every_rows = lax.all_gather(owner_rows, "dp", axis=1, tiled=True)
    delta = rows_at(every_rows, slots)
    weight_delta = delta.reshape(matrices, local_rows, features)
    return (weight_delta, first_out, second_out)


def solution(mesh):
    return jax.shard_map(
        shards,
        mesh=mesh,
        in_specs=(
            P("dp", None, "fsdp", None),
            P(None, "fsdp", None),
            P(None, "fsdp"),
            P(None, "fsdp", "dp", None, None),
            P(None, "fsdp", "dp", None, None),
        ),
        out_specs=(
            P(None, "fsdp", None),
            P(None, "fsdp", "dp", None, None),
            P(None, "fsdp", "dp", None, None),
        ),
        check_vma=False,
    )
```

profile of v0, /device:TPU:1, one launch (start us, length us, event | category | flops | bytes accessed | tf_op | source)
XLA Modules:
  0.0 785.3 jit_solution(841170741054117501)
XLA Ops:
  7.2 4.3 fusion.70
  11.8 96.7 %all-reduce.4.cloned.1.call-done = f32[2,512,512]{1,2,0:T(8,128)} async-done(((f32[2,512,512]{1,2,0:T(8,128)}), f32[2,512,512]{1,2,0:T(8,128)}) %all-reduce.4.cloned.1.call-update) | async-done | bytes 2097168 | tf_op jit(solution)/shard_map/psum | solution.py:33
  108.4 3.0 copy.48
  114.9 23.5 %custom-call.34 = f32[2,128,128]{2,1,0:T(8,128)S(1)} custom-call(f32[2,128,128]{2,1,0:T(8,128)S(1)} %cholesky.274), custom_call_target="Cholesky" | custom-call | tf_op jit(solution)/shard_map/jit(cholesky)/cholesky | solution.py:34
  138.4 19.7 %custom-call.35 = f32[2,1,128,128]{2,3,1,0:T(8,128)S(1)} custom-call(f32[2,1,128,128]{3,2,1,0:T(8,128)S(1)} %select_bitcast_fusion.2), custom_call_target="InvertDiagBlocksLowerTriangular" | custom-call | tf_op jit(solution)/shard_map/jit(cholesky)/cholesky | solution.py:34
  161.4 23.5 %custom-call.36 = f32[2,128,128]{2,1,0:T(8,128)S(1)} custom-call(f32[2,128,128]{2,1,0:T(8,128)S(1)} %cholesky.278), custom_call_target="Cholesky" | custom-call | tf_op jit(solution)/shard_map/jit(cholesky)/cholesky | solution.py:34
  184.9 19.8 %custom-call.37 = f32[2,1,128,128]{2,3,1,0:T(8,128)S(1)} custom-call(f32[2,1,128,128]{3,2,1,0:T(8,128)S(1)} %get-tuple-element.32), custom_call_target="InvertDiagBlocksLowerTriangular" | custom-call | tf_op jit(solution)/shard_map/jit(cholesky)/cholesky | solution.py:34
  206.7 23.5 %custom-call.38 = f32[2,128,128]{2,1,0:T(8,128)S(1)} custom-call(f32[2,128,128]{2,1,0:T(8,128)S(1)} %cholesky.283), custom_call_target="Cholesky" | custom-call | tf_op jit(solution)/shard_map/jit(cholesky)/cholesky | solution.py:34
  230.2 19.7 %custom-call.39 = f32[2,1,128,128]{2,3,1,0:T(8,128)S(1)} custom-call(f32[2,1,128,128]{3,2,1,0:T(8,128)S(1)} %get-tuple-element.30), custom_call_target="InvertDiagBlocksLowerTriangular" | custom-call | tf_op jit(solution)/shard_map/jit(cholesky)/cholesky | solution.py:34
  251.7 23.7 %custom-call.40 = f32[2,128,128]{2,1,0:T(8,128)S(1)} custom-call(f32[2,128,128]{2,1,0:T(8,128)S(1)} %convolution_subtract_fusion.4), custom_call_target="Cholesky" | custom-call | tf_op jit(solution)/shard_map/jit(cholesky)/cholesky | solution.py:34
  277.4 14.9 %while.1 = (s32[]{:T(128)}, f32[2,512,512]{2,1,0:T(8,128)}, s32[4,2]{0,1:T(2,128)S(1)}, f32[4,2,128,128]{3,2,0,1:T(8,128)}, s32[]{:T(128)}) while((s32[]{:T(128)}, f32[2,512,512]{2,1,0:T(8,128)}, s32[4,2]{0,1:T(2,128)S(1)}, f32[4,2,128,128]{3,2,0,1:T(8,128)}, s32[]{:T(128)}) %tuple.37), condition=%wide.while_cond, body=%wide.while_body.sunk | while | flops 2 | bytes 263777 | solution.py:35
  278.1 3.1 bitcast_dynamic-update-slice_fusion.2
  281.9 3.1 bitcast_dynamic-update-slice_fusion.2
  285.6 3.1 bitcast_dynamic-update-slice_fusion.2
  289.3 3.0 bitcast_dynamic-update-slice_fusion.2
  292.3 79.4 %custom-call.41 = f32[2,4,128,128]{2,3,1,0:T(8,128)S(1)} custom-call(f32[2,4,128,128]{3,2,1,0:T(8,128)} %bitcast.129), custom_call_target="InvertDiagBlocksLowerTriangular" | custom-call | tf_op jit(solution)/shard_map/triangular_solve | solution.py:35
  378.9 62.6 %all-gather.3.cloned.1.call-done = bf16[2,1024,512]{1,2,0:T(8,128)(2,1)} async-done(((bf16[2,128,512]{1,2,0:T(8,128)(2,1)}), bf16[2,1024,512]{1,2,0:T(8,128)(2,1)}) %all-gather.3.cloned.1.call-update) | async-done | bytes 2097168 | tf_op jit(solution)/shard_map/all_gather | solution.py:38
  441.5 7.2 fusion.2
  448.7 5.4 copy.63
  455.4 235.6 %all-reduce.6.cloned.1.call-done = f32[2,64,16,512]{3,2,1,0:T(8,128)} async-done(((f32[2,64,16,512]{3,2,1,0:T(8,128)}), f32[2,64,16,512]{3,2,1,0:T(8,128)}) %all-reduce.6.cloned.1.call-update) | async-done | bytes 4194320 | tf_op jit(solution)/shard_map/psum | solution.py:53
  691.0 2.8 gather_fusion
  696.7 71.6 %all-gather.5.cloned.1.call-done = bf16[2,128,16,1024]{3,2,1,0:T(8,128)(2,1)} async-done(((bf16[2,4,16,1024]{3,2,1,0:T(8,128)(2,1)}), bf16[2,128,16,1024]{3,2,1,0:T(8,128)(2,1)}) %all-gather.5.cloned.1.call-update) | async-done | bytes 8388624 | tf_op jit(solution)/shard_map/all_gather | solution.py:65
  768.3 6.3 gather_fusion.1
  774.5 3.9 bitcast_select_fusion
  (78 shorter events, 26.6 us)
Async XLA Ops:
  7.2 101.3 %all-reduce.4.cloned.1.call-start = ((), (), s32[]{:S(2)}) async-start(), calls=%async_computation | async-start | bytes 4194304 | tf_op jit(solution)/shard_map/psum | solution.py:33
  11.6 429.9 %all-gather.3.cloned.1.call-start = ((), (), s32[]{:S(2)}) async-start(), calls=%async_computation.1 | async-start | bytes 2359296 | tf_op jit(solution)/shard_map/all_gather | solution.py:38
  108.4 3.0 copy-start
  113.6 1.3 copy-start.1
  275.7 96.1 %copy-start.2 = (f32[2,128,512]{2,1,0:T(8,128)S(1)}, f32[2,128,512]{2,1,0:T(8,128)}, u32[]{:S(2)}) copy-start(f32[2,128,512]{2,1,0:T(8,128)} %param.6) | copy-start | bytes 1572868
  378.9 312.2 %all-reduce.6.cloned.1.call-start = ((), (), s32[]{:S(2)}) async-start(), calls=%async_computation.2 | async-start | bytes 8388608 | tf_op jit(solution)/shard_map/psum | solution.py:53
  454.1 0.7 copy-start.6
  454.1 239.6 %copy-start.3 = (bf16[2,1024,512]{1,2,0:T(8,128)(2,1)S(1)}, bf16[2,1024,512]{1,2,0:T(8,128)(2,1)}, u32[]{:S(2)}) copy-start(bf16[2,1024,512]{1,2,0:T(8,128)(2,1)} %all-gather.3.cloned.1.call-done) | copy-start | bytes 6291460
  454.2 239.6 %copy-start.4 = (f32[2,1,4,16,512]{4,3,2,1,0:T(8,128)S(1)}, f32[2,1,4,16,512]{4,3,2,1,0:T(8,128)}, u32[]{:S(2)}) copy-start(f32[2,1,4,16,512]{4,3,2,1,0:T(8,128)} %param.9) | copy-start | bytes 786436
  454.2 239.6 %copy-start.5 = (f32[2,1,4,16,512]{4,3,2,1,0:T(8,128)S(1)}, f32[2,1,4,16,512]{4,3,2,1,0:T(8,128)}, u32[]{:S(2)}) copy-start(f32[2,1,4,16,512]{4,3,2,1,0:T(8,128)} %param.8) | copy-start | bytes 786436
  454.2 314.1 %all-gather.5.cloned.1.call-start = ((), (), s32[]{:S(2)}) async-start(), calls=%async_computation.3 | async-start | bytes 8650752 | tf_op jit(solution)/shard_map/all_gather | solution.py:65
Sparse Core Ops, SparseCore 0:
  11.7 96.6 all-reduce.3
  379.0 62.5 all-gather.2
  454.3 236.6 all-reduce.5
  695.3 72.9 all-gather.4
where the time goes:
time: 796 us; the launch traced here: 785 us
  waiting for transfers between devices  467 us (59%)
  other arithmetic  243 us (31%)
  local copies, waits for them, and re-layouts  35 us (4%)
  matrix products  26 us (3%)
  between operations  14.5 us (2%)
    psum x1, waiting for transfers between devices, shards(): totals = lax.psum(blocks, 'dp')  236 us
    another operation x16, other arithmetic, shards(): factor = jnp.linalg.cholesky(gram)  154 us
    psum x1, waiting for transfers between devices, shards(): gram = lax.psum(gram_part, 'fsdp')  96.7 us
    another operation x5, other arithmetic, shards(): lax.linalg.triangular_solve(factor, raw_proj, left_side=False, lower=True...  82 us
    all_gather x1, waiting for transfers between devices, shards(): every_rows = lax.all_gather(owner_rows, 'dp', axis=1, tiled=True)  71.6 us
    all_gather x1, waiting for transfers between devices, shards(): lax.all_gather(basis_part.astype(jnp.bfloat16), 'fsdp', axis=1, tiled=True)  62.6 us
  transfers between devices with their start and end apart: 4, of which 4 were waited for; matrix products, arithmetic and copies ran while one was open for 0% of the time, Pallas kernels for 0%

commit v1 on v0

--- a/solution.py
+++ b/solution.py
@@ -62,7 +62,15 @@
     owner_rows = jnp.einsum(
         "mcbr,mkr->mcbk", update, basis, preferred_element_type=jnp.float32
     ).astype(jnp.bfloat16)
-    every_rows = lax.all_gather(owner_rows, "dp", axis=1, tiled=True)
+    every_rows = jnp.concatenate(
+        jax.lax.all_to_all(
+            jnp.stack([owner_rows] * jax.lax.axis_size("dp")),
+            axis_name="dp",
+            split_axis=0,
+            concat_axis=0,
+        ),
+        axis=1,
+    )
     delta = rows_at(every_rows, slots)
     weight_delta = delta.reshape(matrices, local_rows, features)
     return (weight_delta, first_out, second_out)

time: 796 us -> 929 us (1.17)
  waiting for transfers between devices: 467 us -> 580 us
  local copies, waits for them, and re-layouts: 35 us -> 48 us
    all_to_all x0 -> x1, waiting for transfers between devices: none -> 185 us  [shards(): jax.lax.all_to_all(jnp.stack([owner_rows] * jax.lax.axis_size('dp')), axi...]
    all_gather x1 -> x0, waiting for transfers between devices: 71.6 us -> none  [shards(): every_rows = lax.all_gather(owner_rows, 'dp', axis=1, tiled=True)]
    another operation x12 -> x13, local copies, waits for them, and re-layouts: 14.9 us -> 19.2 us
where the time goes in v1:
time: 929 us; the launch traced here: 918 us
  waiting for transfers between devices  580 us (62%)
  other arithmetic  243 us (26%)
  local copies, waits for them, and re-layouts  48 us (5%)
  matrix products  25.3 us (3%)
  between operations  14.3 us (2%)
    psum x1, waiting for transfers between devices, shards(): totals = lax.psum(blocks, 'dp')  236 us
    all_to_all x1, waiting for transfers between devices, shards(): jax.lax.all_to_all(jnp.stack([owner_rows] * jax.lax.axis_size('dp')), axi...  185 us
    another operation x16, other arithmetic, shards(): factor = jnp.linalg.cholesky(gram)  154 us
    psum x1, waiting for transfers between devices, shards(): gram = lax.psum(gram_part, 'fsdp')  96.6 us
    another operation x5, other arithmetic, shards(): lax.linalg.triangular_solve(factor, raw_proj, left_side=False, lower=True...  82 us
    all_gather x1, waiting for transfers between devices, shards(): lax.all_gather(basis_part.astype(jnp.bfloat16), 'fsdp', axis=1, tiled=True)  62.6 us
  transfers between devices with their start and end apart: 4, of which 4 were waited for; matrix products, arithmetic and copies ran while one was open for 0% of the time, Pallas kernels for 0%

profile of v1, /device:TPU:1, one launch (start us, length us, event | category | flops | bytes accessed | tf_op | source)
XLA Modules:
  0.0 918.3 jit_solution(2003758061917355047)
XLA Ops:
  7.2 4.4 fusion.70
  11.8 96.6 %all-reduce.4.cloned.1.call-done = f32[2,512,512]{1,2,0:T(8,128)} async-done(((f32[2,512,512]{1,2,0:T(8,128)}), f32[2,512,512]{1,2,0:T(8,128)}) %all-reduce.4.cloned.1.call-update) | async-done | bytes 2097168 | tf_op jit(solution)/shard_map/psum | solution.py:33
  114.9 23.5 %custom-call.34 = f32[2,128,128]{2,1,0:T(8,128)S(1)} custom-call(f32[2,128,128]{2,1,0:T(8,128)S(1)} %cholesky.274), custom_call_target="Cholesky" | custom-call | tf_op jit(solution)/shard_map/jit(cholesky)/cholesky | solution.py:34
  138.4 19.7 %custom-call.35 = f32[2,1,128,128]{2,3,1,0:T(8,128)S(1)} custom-call(f32[2,1,128,128]{3,2,1,0:T(8,128)S(1)} %select_bitcast_fusion.2), custom_call_target="InvertDiagBlocksLowerTriangular" | custom-call | tf_op jit(solution)/shard_map/jit(cholesky)/cholesky | solution.py:34
  161.3 23.5 %custom-call.36 = f32[2,128,128]{2,1,0:T(8,128)S(1)} custom-call(f32[2,128,128]{2,1,0:T(8,128)S(1)} %cholesky.278), custom_call_target="Cholesky" | custom-call | tf_op jit(solution)/shard_map/jit(cholesky)/cholesky | solution.py:34
  184.8 20.1 %custom-call.37 = f32[2,1,128,128]{2,3,1,0:T(8,128)S(1)} custom-call(f32[2,1,128,128]{3,2,1,0:T(8,128)S(1)} %get-tuple-element.32), custom_call_target="InvertDiagBlocksLowerTriangular" | custom-call | tf_op jit(solution)/shard_map/jit(cholesky)/cholesky | solution.py:34
  206.9 23.5 %custom-call.38 = f32[2,128,128]{2,1,0:T(8,128)S(1)} custom-call(f32[2,128,128]{2,1,0:T(8,128)S(1)} %cholesky.283), custom_call_target="Cholesky" | custom-call | tf_op jit(solution)/shard_map/jit(cholesky)/cholesky | solution.py:34
  230.4 19.7 %custom-call.39 = f32[2,1,128,128]{2,3,1,0:T(8,128)S(1)} custom-call(f32[2,1,128,128]{3,2,1,0:T(8,128)S(1)} %get-tuple-element.30), custom_call_target="InvertDiagBlocksLowerTriangular" | custom-call | tf_op jit(solution)/shard_map/jit(cholesky)/cholesky | solution.py:34
  251.9 23.6 %custom-call.40 = f32[2,128,128]{2,1,0:T(8,128)S(1)} custom-call(f32[2,128,128]{2,1,0:T(8,128)S(1)} %convolution_subtract_fusion.4), custom_call_target="Cholesky" | custom-call | tf_op jit(solution)/shard_map/jit(cholesky)/cholesky | solution.py:34
  277.7 14.9 %while.1 = (s32[]{:T(128)}, f32[2,512,512]{2,1,0:T(8,128)}, s32[4,2]{0,1:T(2,128)S(1)}, f32[4,2,128,128]{3,2,0,1:T(8,128)}, s32[]{:T(128)}) while((s32[]{:T(128)}, f32[2,512,512]{2,1,0:T(8,128)}, s32[4,2]{0,1:T(2,128)S(1)}, f32[4,2,128,128]{3,2,0,1:T(8,128)}, s32[]{:T(128)}) %tuple.37), condition=%wide.while_cond, body=%wide.while_body.sunk | while | flops 2 | bytes 263777 | solution.py:35
  278.3 3.1 bitcast_dynamic-update-slice_fusion.2
  282.1 3.1 bitcast_dynamic-update-slice_fusion.2
  285.8 3.1 bitcast_dynamic-update-slice_fusion.2
  292.6 79.4 %custom-call.41 = f32[2,4,128,128]{2,3,1,0:T(8,128)S(1)} custom-call(f32[2,4,128,128]{3,2,1,0:T(8,128)} %bitcast.133), custom_call_target="InvertDiagBlocksLowerTriangular" | custom-call | tf_op jit(solution)/shard_map/triangular_solve | solution.py:35
  379.1 62.6 %all-gather.2.cloned.1.call-done = bf16[2,1024,512]{1,2,0:T(8,128)(2,1)} async-done(((bf16[2,128,512]{1,2,0:T(8,128)(2,1)}), bf16[2,1024,512]{1,2,0:T(8,128)(2,1)}) %all-gather.2.cloned.1.call-update) | async-done | bytes 2097168 | tf_op jit(solution)/shard_map/all_gather | solution.py:38
  441.8 7.2 fusion.2
  449.0 5.6 copy.86
  455.8 235.7 %all-reduce.6.cloned.1.call-done = f32[2,64,16,512]{3,2,1,0:T(8,128)} async-done(((f32[2,64,16,512]{3,2,1,0:T(8,128)}), f32[2,64,16,512]{3,2,1,0:T(8,128)}) %all-reduce.6.cloned.1.call-update) | async-done | bytes 4194320 | tf_op jit(solution)/shard_map/psum | solution.py:53
  694.9 4.3 stack.2
  699.2 7.1 all-to-all-start
  707.8 185.1 %all-to-all-done = bf16[32,2,4,16,1024]{4,3,2,1,0:T(8,128)(2,1)} async-done(((bf16[32,2,4,16,1024]{4,3,2,1,0:T(8,128)(2,1)}), bf16[32,2,4,16,1024]{4,3,2,1,0:T(8,128)(2,1)}, u32[]{:S(2)}, u32[]{:S(2)}) %all-to-all-start) | async-done | bytes 8388640 | tf_op jit(solution)/shard_map/all_to_all | solution.py:66
  892.9 8.5 copy.89
  901.4 6.3 gather_fusion.1
  907.7 3.9 bitcast_select_fusion
  (79 shorter events, 34.7 us)
Async XLA Ops:
  7.2 101.3 %all-reduce.4.cloned.1.call-start = ((), (), s32[]{:S(2)}) async-start(), calls=%async_computation.1 | async-start | bytes 4194304 | tf_op jit(solution)/shard_map/psum | solution.py:33
  11.6 430.2 %all-gather.2.cloned.1.call-start = ((), (), s32[]{:S(2)}) async-start(), calls=%async_computation.2 | async-start | bytes 2359296 | tf_op jit(solution)/shard_map/all_gather | solution.py:38
  108.4 3.0 copy-start
  113.5 1.3 copy-start.1
  275.9 96.1 %copy-start.2 = (f32[2,128,512]{2,1,0:T(8,128)S(1)}, f32[2,128,512]{2,1,0:T(8,128)}, u32[]{:S(2)}) copy-start(f32[2,128,512]{2,1,0:T(8,128)} %param.6) | copy-start | bytes 1572868
  379.1 312.4 %all-reduce.6.cloned.1.call-start = ((), (), s32[]{:S(2)}) async-start(), calls=%async_computation.3 | async-start | bytes 8388608 | tf_op jit(solution)/shard_map/psum | solution.py:53
  454.6 0.7 copy-start.6
  454.6 239.7 %copy-start.3 = (bf16[2,1024,512]{1,2,0:T(8,128)(2,1)S(1)}, bf16[2,1024,512]{1,2,0:T(8,128)(2,1)}, u32[]{:S(2)}) copy-start(bf16[2,1024,512]{1,2,0:T(8,128)(2,1)} %all-gather.2.cloned.1.call-done) | copy-start | bytes 6291460
  454.6 239.7 %copy-start.4 = (f32[2,1,4,16,512]{4,3,2,1,0:T(8,128)S(1)}, f32[2,1,4,16,512]{4,3,2,1,0:T(8,128)}, u32[]{:S(2)}) copy-start(f32[2,1,4,16,512]{4,3,2,1,0:T(8,128)} %param.9) | copy-start | bytes 786436
  454.6 239.7 %copy-start.5 = (f32[2,1,4,16,512]{4,3,2,1,0:T(8,128)S(1)}, f32[2,1,4,16,512]{4,3,2,1,0:T(8,128)}, u32[]{:S(2)}) copy-start(f32[2,1,4,16,512]{4,3,2,1,0:T(8,128)} %param.8) | copy-start | bytes 786436
  699.2 193.7 %all-to-all-start = ((bf16[32,2,4,16,1024]{4,3,2,1,0:T(8,128)(2,1)}), bf16[32,2,4,16,1024]{4,3,2,1,0:T(8,128)(2,1)}, u32[]{:S(2)}, u32[]{:S(2)}) async-start(bf16[32,2,4,16,1024]{4,3,2,1,0:T(8,128)(2,1)} %stack.2), calls=%async_computation | async-start | bytes 16777216 | tf_op jit(solution)/shard_map/all_to_all | solution.py:66
Sparse Core Ops, SparseCore 0:
  11.7 96.6 all-reduce.3
  379.2 62.5 all-gather.1
  454.7 236.6 all-reduce.5
